TPU v7x, 256 devices: a whole 4x4x8 slice. The times are simulated.
256 devices in a mesh: section: 4 (over x_hi, core), seq: 64 (over z, x_lo, y).
Axes of the slice: x: 4 (x_hi: 2, x_lo: 2; x = x_hi * 2 + x_lo), y: 4, z: 8, core: 2. Of those that a mesh axis runs over, the one named last changes fastest.
Arguments:
- x_in: bfloat16 [2, 64, 128, 2048], P(None, 'seq'), may hold values from -6 to 6
- x_tan: bfloat16 [2, 64, 128, 2048], P(None, 'seq'), may hold values from -6 to 6
- t_index: int32 [2], replicated, may hold values from 0 to 999
- w_qkv: bfloat16 [4, 2048, 3072], P('section', 'seq'), may hold values from -0.125 to 0.125
- w_out: bfloat16 [4, 1024, 2048], P('section', 'seq'), may hold values from -0.1875 to 0.1875
- qk_gain: float32 [4, 2, 128], P('section'), may hold values from 0.1 to 1.9
- mod_amp: float32 [4, 3, 2048], P('section'), may hold values from -1 to 1
- mod_freq: float32 [4, 3, 2048], P('section'), may hold values from 0.5 to 4
- mod_phase: float32 [4, 3, 2048], P('section'), may hold values from -3.140625 to 3.140625
Outputs:
- section_out: bfloat16 [4, 2, 64, 128, 2048], P('section', None, 'seq')
- section_tan: bfloat16 [4, 2, 64, 128, 2048], P('section', None, 'seq')
All inputs are finite; a program needn't handle non-finite values.
Results may differ from a plain program's by a relative error of at most 0.018.
Values may be sent and summed in bfloat16 or wider, within the bound.
A program may use at most 192 MiB of HBM per device.

v0:
```python
import functools
import math

import jax
import jax.numpy as jnp
from jax import lax
from jax.experimental import pallas as pl
from jax.experimental.pallas import tpu as pltpu
from jax.sharding import PartitionSpec as P

HEADS = 8
HEAD = 128
T_STEPS = 1000
D = 2048
KT = D // HEAD
HD = HEADS * HEAD
F = 64
NP = 2
VIDS = 2
UNITS = VIDS * NP
ROWS = 2 * F
HALF = F
HOP_PARTS = 4
STRIDE = 27
EPS = 1e-06
F32 = jnp.float32
BF16 = jnp.bfloat16
MESH = pl.DeviceIdType.MESH
ROWS_OUT = 16
PACKED = 2 * 3 * HD + D
Z_LAST, Y_LAST = 2560, 5632


def timing(amp, freq, phase, time_value):
    angle = freq * time_value + phase
    return (amp * jnp.sin(angle), amp * freq * jnp.cos(angle))


class Gather:
    def __init__(self, sizes, section, coords, weights, send, recv):
        self.sizes, self.section, self.coords = sizes, section, coords
        self.weights, self.send, self.recv = weights, send, recv
        self.live = []
        self.sems = 0
        self.rings = {}

    def peer(self, axis, by):
        z, xl, y = self.coords
        nz, nx, ny = self.sizes
        if axis == "z":
            z = lax.rem(z + by + nz, nz)
        elif axis == "y":
            y = lax.rem(y + by + ny, ny)
        else:
            xl = nx - 1 - xl
        return (self.section, (z * nx + xl) * ny + y)

    def copy(self, ref, sem, peer):
        return pltpu.make_async_remote_copy(
            src_ref=ref,
            dst_ref=ref,
            send_sem=self.send.at[sem],
            recv_sem=self.recv.at[sem],
            device_id=peer,
            device_id_type=MESH,
        )

    def start(self, copy):
        copy.start()
        self.live.append(copy)

    def ring(self, axis, first, stop, fixed, single=False):
        size = self.sizes[0] if axis == "z" else self.sizes[2]
        me = self.coords[0] if axis == "z" else self.coords[2]
        last = size // 2
        first_sem = self.sems
        self.sems += 2 * last

        def copy(way, step, index):
            z, y = (index, fixed) if axis == "z" else (fixed, index)
            begin, width = first, stop - first
            xl = self.coords[1] if single else slice(None)
            if step == last - 1:
                if single:
                    width = width // 2
                    begin = begin + way * width
                else:
                    xl = way
            ref = self.weights.at[z, xl, y, :, pl.ds(begin, width)]
            return self.copy(ref, first_sem + 2 * step + way, self.peer(axis, 1 - 2 * way))

        def at(way, step):
            return lax.rem(me - (1 - 2 * way) * step + size, size)

        for step in range(last):
            for way in (0, 1):
                self.start(copy(way, step, at(way, step)))
            yield
            for way in (0, 1):
                copy(way, step, at(way, step + 1)).wait_recv()

    def beside(self, fixed):
        sem = self.sems
        self.sems += 1
        columns = pl.ds(Y_LAST, PACKED - Y_LAST)
        _, xl, _ = self.coords
        nx = self.sizes[1]
        self.start(
            self.copy(self.weights.at[fixed, xl, :, :, columns], sem, self.peer("x", 0))
        )
        yield
        self.copy(
            self.weights.at[fixed, nx - 1 - xl, :, :, columns], sem, self.peer("x", 0)
        ).wait_recv()

    def build(self):
        z, _, y = self.coords
        nz, _, ny = self.sizes
        rings = self.rings
        rings["a"] = self.ring("y", 0, Z_LAST, z)
        rings["b"] = self.ring("z", Z_LAST, Y_LAST, y)
        rings["c"] = self.ring("z", Y_LAST, PACKED, y, True)
        for by in range(ny):
            rings["az", by] = self.ring("z", 0, Z_LAST, lax.rem(y + by, ny))
        for by in range(nz):
            there = lax.rem(z + by, nz)
            rings["by", by] = self.ring("y", Z_LAST, Y_LAST, there)
            rings["cy", by] = self.ring("y", Y_LAST, PACKED, there, True)
            rings["cx", by] = self.beside(there)

    def go(self, *names):
        for name in names:
            next(self.rings[name], None)

    def finish(self):
        for copy in self.live:
            copy.wait_send()


def spread(source, tall, start):
    count = source.shape[0]
    for k in range(KT):
        tall[pl.ds(start + k, count, stride=KT), :] = source[:, k * HEAD : (k + 1) * HEAD].astype(
            F32
        )


def normalize(values, tangents, gain):
    inverse = lax.rsqrt(jnp.mean(values * values, axis=-1, keepdims=True) + EPS)
    cross = jnp.mean(values * tangents, axis=-1, keepdims=True)
    scaled = values * inverse
    return (
        (scaled * gain).astype(BF16),
        ((inverse * tangents - values * inverse**3 * cross) * gain).astype(BF16),
    )


def attend(q2, k2, v2, gains_ref):
    factor = 1.0 / math.sqrt(HEAD)
    qn, dqn = normalize(q2[:HALF], q2[HALF:], gains_ref[0:1, :])
    kn, dkn = normalize(k2[:HALF], k2[HALF:], gains_ref[1:2, :])
    value, dvalue = v2[:HALF].astype(BF16), v2[HALF:].astype(BF16)

    def against(rows, columns):
        return lax.dot_general(
            rows, columns, (((1,), (1,)), ((), ())), preferred_element_type=F32
        )

    scores = against(jnp.concatenate([qn, dqn], axis=0), kn)
    score = scores[:HALF] * factor
    dscore = (scores[HALF:] + against(qn, dkn)) * factor
    expo = jnp.exp(score)
    prob = expo * (1.0 / jnp.sum(expo, axis=-1, keepdims=True))
    growth = prob * dscore
    dprob = growth - prob * jnp.sum(growth, axis=-1, keepdims=True)
    prob, dprob = prob.astype(BF16), dprob.astype(BF16)
    mixed = jnp.dot(
        jnp.concatenate([prob, dprob], axis=0), value, preferred_element_type=F32
    )
    return mixed[:HALF], mixed[HALF:] + jnp.dot(prob, dvalue, preferred_element_type=F32)


def block_step(
    unit, entering, leaving, weights, gains_ref, mods_ref, dmods_ref, tall, flat, att
):
    group = 8
    vid = unit // NP

    @pl.loop(0, F // group, unroll=2)
    def _(i):
        first = pl.multiple_of(i * group, group)
        hidden = entering[unit, pl.ds(first, group), 0].astype(F32)
        tangent = entering[unit, pl.ds(first, group), 1].astype(F32)

        def mean(values):
            return jnp.sum(
                jnp.sum(values, axis=1, keepdims=True), axis=2, keepdims=True
            ) * (1.0 / D)

        inverse = lax.rsqrt(mean(hidden * hidden) + EPS)
        cross = mean(hidden * tangent)
        normed = hidden * inverse
        dnormed = inverse * tangent - hidden * inverse**3 * cross
        scale = 1.0 + mods_ref[vid, 1][None]
        modulated = normed * scale + mods_ref[vid, 0][None]
        dmodulated = dnormed * scale + normed * dmods_ref[vid, 1][None] + dmods_ref[vid, 0][None]
        row = pl.multiple_of(first * KT, group * KT)
        tall[pl.ds(row, group * KT), :] = modulated.reshape(group * KT, HEAD)
        tall[pl.ds(row + HALF * KT, group * KT), :] = dmodulated.reshape(group * KT, HEAD)

    for k in range(KT):
        flat[:, k * HEAD : (k + 1) * HEAD] = tall[pl.ds(k, ROWS, stride=KT), :].astype(BF16)

    def third(number, pair):
        column = number * HD + pair * 2 * HEAD
        halves = [
            weights[
                :, :, :, :, column + lower * 3 * HD : column + lower * 3 * HD + 2 * HEAD
            ].reshape(F, 1, ROWS_OUT, 2 * HEAD)
            for lower in range(2)
        ]
        matrix = jnp.concatenate(halves, axis=1).reshape(D, 2 * HEAD)
        return jnp.dot(flat[...], matrix, preferred_element_type=F32)

    ahead = [third(number, 0) for number in range(3)]
    for pair in range(HEADS // 2):
        q2, k2, v2 = ahead
        if pair + 1 < HEADS // 2:
            ahead = [third(number, pair + 1) for number in range(3)]
        for one in range(2):
            lanes = slice(one * HEAD, (one + 1) * HEAD)
            output, doutput = attend(q2[:, lanes], k2[:, lanes], v2[:, lanes], gains_ref)
            column = (pair * 2 + one) * HEAD
            att[:HALF, column : column + HEAD] = output.astype(BF16)
            att[HALF:, column : column + HEAD] = doutput.astype(BF16)

    for n in range(KT // 2):
        column = 2 * 3 * HD + n * 2 * HEAD
        matrix = weights[:, :, :, :, column : column + 2 * HEAD].reshape(HD, 2 * HEAD)
        y = jnp.dot(att[...], matrix, preferred_element_type=F32)
        tall[pl.ds(2 * n, ROWS, stride=KT), :] = y[:, :HEAD]
        tall[pl.ds(2 * n + 1, ROWS, stride=KT), :] = y[:, HEAD:]

    @pl.loop(0, F // group, unroll=2)
    def _(i):
        first = pl.multiple_of(i * group, group)
        row = pl.multiple_of(first * KT, group * KT)
        y = tall[pl.ds(row, group * KT), :].reshape(group, KT, HEAD)
        dy = tall[pl.ds(row + HALF * KT, group * KT), :].reshape(group, KT, HEAD)
        hidden = entering[unit, pl.ds(first, group), 0].astype(F32)
        tangent = entering[unit, pl.ds(first, group), 1].astype(F32)
        gate = mods_ref[vid, 2][None]
        dgate = dmods_ref[vid, 2][None]
        leaving[unit, pl.ds(first, group), 0] = (hidden + gate * y).astype(BF16)
        leaving[unit, pl.ds(first, group), 1] = (tangent + dgate * y + gate * dy).astype(BF16)


def kernel(
    sizes,
    sections,
    x_ref,
    t_ref,
    wqkv_ref,
    wout_ref,
    gains_ref,
    index_ref,
    amp_ref,
    freq_ref,
    phase_ref,
    out_ref,
    tan_ref,
    weights,
    mods_ref,
    dmods_ref,
    plain,
    staged,
    relay,
    entering,
    leaving,
    returned,
    tall,
    flat,
    att,
    load_sem,
    own_sem,
    swap_send,
    swap_recv,
    ring_send,
    ring_recv,
    x_send,
    x_recv,
    relay_send,
    relay_recv,
    pass_send,
    pass_recv,
    out_send,
    out_recv,
    turn_sem,
):
    nz, nx, ny = sizes
    count = nz * nx * ny
    section = lax.axis_index("section")
    me = lax.axis_index("seq")
    coords = (me // (nx * ny), (me // ny) % nx, me % ny)
    z, xl, y = coords
    first_half = section < 2

    def flip(index):
        return index + ny - 2 * ny * ((index // ny) % nx)

    across = flip(me)
    slot = jnp.where(first_half, me, across)
    neighbour = (section, lax.rem(me + 1, count))
    group = 8

    def exchange(source, row_of, target, place, send, recv):
        pltpu.make_async_copy(source.at[row_of(me)], target.at[place], recv).start()

        @pl.loop(1, count, unroll=7)
        def _(by):
            to = lax.rem(me + by * STRIDE, count)
            pltpu.make_async_remote_copy(
                src_ref=source.at[row_of(to)],
                dst_ref=target.at[place],
                send_sem=send,
                recv_sem=recv,
                device_id=(section, to),
                device_id_type=MESH,
            ).start()

    def exchange_came(source, target, recv):
        pltpu.make_async_copy(source, target, recv).wait()

    def exchange_sent(source, target, send, recv):
        pltpu.make_async_remote_copy(
            src_ref=source.at[pl.ds(0, count - 1)],
            dst_ref=target.at[pl.ds(0, count - 1)],
            send_sem=send,
            recv_sem=recv,
            device_id=neighbour,
            device_id_type=MESH,
        ).wait_send()

    leads = lax.rem(section, 2) == 0
    loads = [
        pltpu.make_async_copy(ref, plain.at[tan], load_sem.at[tan])
        for tan, ref in enumerate((x_ref, t_ref))
    ]

    @pl.when(leads)
    def _():
        for load in loads:
            load.start()

    own = []
    for part, (ref, first, width) in enumerate(
        (
            (wqkv_ref.at[pl.ds(0, ROWS_OUT)], 0, 3 * HD),
            (wqkv_ref.at[pl.ds(ROWS_OUT, ROWS_OUT)], 3 * HD, 3 * HD),
            (wout_ref, 6 * HD, D),
        )
    ):
        home = weights.at[z, xl, y, :, pl.ds(first, width)]
        own.append(pltpu.make_async_copy(ref, home, own_sem.at[part]))
        own[-1].start()
    for copy in own:
        copy.wait()

    @pl.when(jnp.logical_not(leads))
    def _():
        pl.semaphore_wait(turn_sem, 1)

    gather = Gather(sizes, section, coords, weights, ring_send, ring_recv)
    gather.build()
    go = gather.go
    mine = weights.at[z, xl, y, :, pl.ds(0, Y_LAST)]
    swap = pltpu.make_async_remote_copy(
        src_ref=mine,
        dst_ref=mine,
        send_sem=swap_send,
        recv_sem=swap_recv,
        device_id=(section, across),
        device_id_type=MESH,
    )
    theirs = weights.at[z, nx - 1 - xl, y, :, pl.ds(0, Y_LAST)]
    swapped = pltpu.make_async_remote_copy(
        src_ref=theirs,
        dst_ref=theirs,
        send_sem=swap_send,
        recv_sem=swap_recv,
        device_id=(section, across),
        device_id_type=MESH,
    )
    swap.start()
    go("c", ("cy", 0))

    def prepare(vid):
        for tan in range(2):
            spread(plain.at[tan, vid], tall, 0)

            @pl.loop(0, count // group)
            def _(i):
                first = pl.multiple_of(i * group, group)
                row = pl.multiple_of(first * NP * KT, group * NP * KT)
                tiles = (
                    tall[pl.ds(row, group * NP * KT), :]
                    .astype(BF16)
                    .reshape(group, NP, KT, HEAD)
                )
                for pos in range(NP):
                    staged[vid * NP + pos, pl.ds(first, group), tan] = tiles[:, pos]

    @pl.when(leads)
    def _():
        for load in loads:
            load.wait()
        prepare(0)

    @pl.when(section == 0)
    def _():
        exchange(
            staged.at[0], lambda f: f, entering.at[0], me, x_send.at[0], x_recv.at[0]
        )

    def second_round(unit):
        exchange(
            staged.at[unit], flip, relay.at[unit], me, x_send.at[unit], x_recv.at[unit]
        )

    @pl.when(section == 2)
    def _():
        second_round(1)
        prepare(1)
        second_round(2)
        second_round(3)

    def relayed(unit):
        return pltpu.make_async_remote_copy(
            src_ref=relay.at[unit],
            dst_ref=entering.at[unit],
            send_sem=relay_send.at[unit],
            recv_sem=relay_recv.at[unit],
            device_id=(0, across),
            device_id_type=MESH,
        )

    def pass_to_first(unit):
        @pl.when(section == 2)
        def _():
            exchange_came(staged.at[unit], relay.at[unit], x_recv.at[unit])
            relayed(unit).start()

    for vid in range(VIDS):
        time_value = (index_ref[vid].astype(F32) + 0.5) * (math.pi / (2.0 * T_STEPS))
        mods_ref[vid], dmods_ref[vid] = timing(
            amp_ref[...], freq_ref[...], phase_ref[...], time_value
        )

    swapped.wait_recv()
    go("b", "a", ("by", 0), ("az", 0))
    go("c", ("cy", 1), ("cy", 7))
    go("a", ("az", 1), ("az", 3))
    go(("cy", 0),)
    go("b", ("by", 1), ("by", 7))
    go("c", ("cy", 2), ("cy", 6))

    @pl.when(leads)
    def _():
        pl.semaphore_signal(
            turn_sem, inc=1, device_id=(section + 1, me), device_id_type=MESH
        )

    go("a", ("az", 2))
    go(("cy", 0), ("cx", 0), ("cy", 1), ("cy", 7))
    go(("az", 0), ("by", 0))
    go("c", ("cy", 3), ("cy", 5))
    go(("cy", 1), ("cx", 1), ("cy", 7), ("cx", 7), ("cy", 2), ("cy", 6))
    go("b", ("by", 2), ("by", 6))
    go("c", ("cy", 4))
    pass_to_first(1)
    go(("az", 1), ("az", 3), ("by", 1), ("by", 7), ("az", 2))
    go(("cy", 2), ("cx", 2), ("cy", 6), ("cx", 6), ("cy", 3), ("cy", 5), ("cy", 4))
    go("b", ("by", 3), ("by", 5))
    go(("az", 0), ("by", 0), ("az", 1), ("az", 3))
    go(("cy", 3), ("cx", 3), ("cy", 5), ("cx", 5), ("cy", 4), ("cx", 4))
    pass_to_first(2)

    go("b", ("by", 4))
    go(("by", 2), ("by", 6), ("az", 2), ("by", 1), ("by", 7), ("az", 0))
    pass_to_first(3)
    go(("by", 3), ("by", 5), ("az", 1), ("az", 3), ("by", 4), ("az", 2))
    go(("by", 2), ("by", 6), ("az", 0), ("by", 3), ("by", 5))
    go(("az", 1), ("az", 3), ("by", 4), ("az", 2))
    go(*(("cx", by) for by in range(nz)))

    @pl.when(section == 1)
    def _():
        pl.semaphore_signal(turn_sem, inc=1, device_id=(0, me), device_id_type=MESH)

    def onward(unit, first=0, frames=F):
        return pltpu.make_async_remote_copy(
            src_ref=leaving.at[unit, pl.ds(first, frames)],
            dst_ref=entering.at[unit, pl.ds(first, frames)],
            send_sem=pass_send.at[unit],
            recv_sem=pass_recv.at[unit],
            device_id=(
                lax.rem(section + 1, sections),
                jnp.where(section == 1, across, me),
            ),
            device_id_type=MESH,
        )

    def send_back(unit):
        exchange(
            leaving.at[unit],
            lambda f: f,
            returned.at[unit],
            slot,
            out_send.at[unit],
            out_recv.at[unit],
        )

    @pl.loop(0, UNITS)
    def _(unit):
        @pl.when(jnp.logical_and(section == 0, unit == 0))
        def _():
            exchange_came(staged.at[0], entering.at[0], x_recv.at[0])

        @pl.when(jnp.logical_and(section == 0, unit > 0))
        def _():
            relayed(unit).wait_recv()

        @pl.when(section > 0)
        def _():
            onward(unit).wait_recv()

        block_step(
            unit, entering, leaving, weights, gains_ref, mods_ref, dmods_ref, tall, flat, att
        )

        @pl.when(section < sections - 1)
        def _():
            for part in range(HOP_PARTS):
                onward(unit, part * (F // HOP_PARTS), F // HOP_PARTS).start()

        @pl.when(section > 0)
        def _():
            send_back(unit)

    @pl.when(section == 0)
    def _():
        pl.semaphore_wait(turn_sem, 1)

        @pl.loop(0, UNITS)
        def _(unit):
            send_back(unit)

    @pl.loop(0, VIDS)
    def _(vid):
        for pos in range(NP):
            unit = vid * NP + pos
            exchange_came(leaving.at[unit], returned.at[unit], out_recv.at[unit])

            @pl.loop(0, count // group)
            def _(i):
                first = pl.multiple_of(i * group, group)
                for tan in range(2):
                    tiles = returned[unit, pl.ds(first, group), tan].astype(F32)
                    for one in range(group):
                        row = pl.multiple_of(
                            ((tan * count + first + one) * NP + pos) * KT, KT
                        )
                        tall[pl.ds(row, KT), :] = tiles[one]

        for tan, result in enumerate((out_ref, tan_ref)):
            for k in range(KT):
                result[vid, :, k * HEAD : (k + 1) * HEAD] = tall[
                    pl.ds(tan * count * NP * KT + k, count * NP, stride=KT), :
                ].astype(BF16)

    gather.finish()
    swap.wait_send()

    @pl.loop(0, UNITS)
    def _(unit):
        exchange_sent(
            leaving.at[unit], returned.at[unit], out_send.at[unit], out_recv.at[unit]
        )

        @pl.when(section < sections - 1)
        def _():
            onward(unit).wait_send()

        @pl.when(
            jnp.logical_or(
                jnp.logical_and(section == 0, unit == 0),
                jnp.logical_and(section == 2, unit > 0),
            )
        )
        def _():
            exchange_sent(
                staged.at[unit], relay.at[unit], x_send.at[unit], x_recv.at[unit]
            )

        @pl.when(jnp.logical_and(section == 2, unit > 0))
        def _():
            relayed(unit).wait_send()


def shards(sizes, x_in, x_tan, t_index, w_qkv, w_out, qk_gain, mod_amp, mod_freq, mod_phase):
    nz, nx, ny = sizes
    count = nz * nx * ny
    sections = lax.axis_size("section")
    places = x_in.shape[2]
    waves = [wave.reshape(3, KT, HEAD) for wave in (mod_amp, mod_freq, mod_phase)]
    outside = pl.BlockSpec(memory_space=pl.ANY)
    inside = pl.BlockSpec(memory_space=pltpu.VMEM)
    result = jax.ShapeDtypeStruct((VIDS, places, D), BF16)
    units = (UNITS, F, 2, KT, HEAD)
    rings = 2 * (ny // 2) * (1 + 2 * nz) + 2 * (nz // 2) * (2 + ny) + nz
    dma = pltpu.SemaphoreType.DMA
    out, tan = pl.pallas_call(
        functools.partial(kernel, sizes, sections),
        out_shape=(result, result),
        in_specs=[outside] * 4
        + [inside, pl.BlockSpec(memory_space=pltpu.SMEM)]
        + [inside] * 3,
        out_specs=(inside, inside),
        scratch_shapes=[
            pltpu.VMEM((nz, nx, ny, ROWS_OUT, PACKED), BF16),
            pltpu.VMEM((VIDS, 3, KT, HEAD), F32),
            pltpu.VMEM((VIDS, 3, KT, HEAD), F32),
            pltpu.VMEM((2, VIDS, places, D), BF16),
            pltpu.VMEM(units, BF16),
            pltpu.VMEM(units, BF16),
            pltpu.VMEM(units, BF16),
            pltpu.VMEM(units, BF16),
            pltpu.VMEM(units, BF16),
            pltpu.VMEM((2 * places * KT, HEAD), F32),
            pltpu.VMEM((ROWS, D), BF16),
            pltpu.VMEM((ROWS, HD), BF16),
            dma((2,)),
            dma((3,)),
            dma,
            dma,
            dma((rings,)),
            dma((rings,)),
            dma((UNITS,)),
            dma((UNITS,)),
            dma((UNITS,)),
            dma((UNITS,)),
            dma((UNITS,)),
            dma((UNITS,)),
            dma((UNITS,)),
            dma((UNITS,)),
            pltpu.SemaphoreType.REGULAR,
        ],
        compiler_params=pltpu.CompilerParams(
            has_side_effects=True, vmem_limit_bytes=60 * 1024 * 1024
        ),
        name="blocks",
    )(
        x_in.reshape(VIDS, places, D),
        x_tan.reshape(VIDS, places, D),
        w_qkv[0],
        w_out[0],
        qk_gain[0],
        t_index,
        *waves,
    )
    return (out[None, :, None], tan[None, :, None])


def solution(mesh):
    count = mesh.shape["seq"]
    sizes = (count // 8, 2, 4)
    placed = (
        P(None, "seq", None, None),
        P(None, "seq", None, None),
        P(),
        P("section", "seq", None),
        P("section", "seq", None),
        P("section", None, None),
        P("section", None, None),
        P("section", None, None),
        P("section", None, None),
    )
    return jax.shard_map(
        functools.partial(shards, sizes),
        mesh=mesh,
        in_specs=placed,
        out_specs=(P("section", None, "seq", None, None), P("section", None, "seq", None, None)),
        check_vma=False,
    )
```

profile of v0, /device:TPU:7, one launch (start us, length us, event | category | flops | bytes accessed | tf_op | source)
XLA Modules:
  0.0 181.2 jit_solution(856495005373534348)
XLA Ops:
  0.6 177.2 %blocks.1 = (bf16[2,128,2048]{2,1,0:T(8,128)(2,1)}, bf16[2,128,2048]{2,1,0:T(8,128)(2,1)}) custom-call(bf16[2,128,2048]{2,1,0:T(8,128)(2,1)} %bitcast.14, bf16[2,128,2048]{2,1,0:T(8,128)(2,1)} %bitcast.15, bf16[32,3072]{1,0:T(8,128)(2,1)} %bitcast.18, bf16[16,2048]{1,0:T(8,128)(2,1)} %bitcast.19, f32[2,128]{1,0:T(2,128)} %bitcast.23, s32[2]{0:T(128)} %index_ref.1, ...), custom_call_target="tpu_custom_call" | custom-call | tf_op jit(solution)/shard_map/blocks/pallas_call | solution.py:622
  177.8 0.0 copy-start
  177.8 2.4 %copy.15 = bf16[1,2,1,128,2048]{4,3,2,1,0:T(8,128)(2,1)} copy(bf16[1,2,1,128,2048]{4,3,2,1,0:T(8,128)(2,1)} %bitcast.17) | data formatting | bytes 2097152
  180.2 0.0 copy-done
  180.2 1.0 copy.16
Async XLA Ops:
  177.8 2.4 %copy-start = (bf16[2,128,2048]{2,1,0:T(8,128)(2,1)S(1)}, bf16[2,128,2048]{2,1,0:T(8,128)(2,1)}, u32[]{:S(2)}) copy-start(bf16[2,128,2048]{2,1,0:T(8,128)(2,1)} %get-tuple-element.5) | copy-start | bytes 3145732
where the time goes:
time: 182 us; the launch traced here: 181 us
  Pallas kernels  177 us (97%)
  local copies, waits for them, and re-layouts  3.37 us (2%)
    pallas_call x1, Pallas kernels, shards(): pl.pallas_call(functools.partial(kernel, sizes, sections), out_shape=(res...  177 us

commit v1 on v0

--- a/solution.py
+++ b/solution.py
@@ -28,7 +28,7 @@
 MESH = pl.DeviceIdType.MESH
 ROWS_OUT = 16
 PACKED = 2 * 3 * HD + D
-Z_LAST, Y_LAST = 2560, 5632
+Z_LAST, Y_LAST = 2816, 5632
 
 
 def timing(amp, freq, phase, time_value):
@@ -65,9 +65,11 @@
             device_id_type=MESH,
         )
 
-    def start(self, copy):
-        copy.start()
-        self.live.append(copy)
+    def start(self, piece, begin, width, sem, peer):
+        for part in range(2):
+            columns = pl.ds(begin + part * (width // 2), width // 2)
+            self.copy(piece(columns), sem, peer).start()
+        self.live.append(self.copy(piece(pl.ds(begin, width)), sem, peer))
 
     def ring(self, axis, first, stop, fixed, single=False):
         size = self.sizes[0] if axis == "z" else self.sizes[2]
@@ -76,7 +78,7 @@
         first_sem = self.sems
         self.sems += 2 * last
 
-        def copy(way, step, index):
+        def arguments(way, step, index):
             z, y = (index, fixed) if axis == "z" else (fixed, index)
             begin, width = first, stop - first
             xl = self.coords[1] if single else slice(None)
@@ -86,32 +88,39 @@
                     begin = begin + way * width
                 else:
                     xl = way
-            ref = self.weights.at[z, xl, y, :, pl.ds(begin, width)]
-            return self.copy(ref, first_sem + 2 * step + way, self.peer(axis, 1 - 2 * way))
+
+            def piece(columns):
+                return self.weights.at[z, xl, y, :, columns]
+
+            return piece, begin, width, first_sem + 2 * step + way, self.peer(axis, 1 - 2 * way)
 
         def at(way, step):
             return lax.rem(me - (1 - 2 * way) * step + size, size)
 
         for step in range(last):
             for way in (0, 1):
-                self.start(copy(way, step, at(way, step)))
+                self.start(*arguments(way, step, at(way, step)))
             yield
             for way in (0, 1):
-                copy(way, step, at(way, step + 1)).wait_recv()
+                piece, begin, width, sem, peer = arguments(way, step, at(way, step + 1))
+                self.copy(piece(pl.ds(begin, width)), sem, peer).wait_recv()
 
     def beside(self, fixed):
         sem = self.sems
         self.sems += 1
-        columns = pl.ds(Y_LAST, PACKED - Y_LAST)
         _, xl, _ = self.coords
         nx = self.sizes[1]
+        peer = self.peer("x", 0)
         self.start(
-            self.copy(self.weights.at[fixed, xl, :, :, columns], sem, self.peer("x", 0))
+            lambda columns: self.weights.at[fixed, xl, :, :, columns],
+            Y_LAST,
+            PACKED - Y_LAST,
+            sem,
+            peer,
         )
         yield
-        self.copy(
-            self.weights.at[fixed, nx - 1 - xl, :, :, columns], sem, self.peer("x", 0)
-        ).wait_recv()
+        columns = pl.ds(Y_LAST, PACKED - Y_LAST)
+        self.copy(self.weights.at[fixed, nx - 1 - xl, :, :, columns], sem, peer).wait_recv()
 
     def build(self):
         z, _, y = self.coords
@@ -186,7 +195,7 @@
     group = 8
     vid = unit // NP
 
-    @pl.loop(0, F // group, unroll=2)
+    @pl.loop(0, F // group, unroll=4)
     def _(i):
         first = pl.multiple_of(i * group, group)
         hidden = entering[unit, pl.ds(first, group), 0].astype(F32)
@@ -241,7 +250,7 @@
         tall[pl.ds(2 * n, ROWS, stride=KT), :] = y[:, :HEAD]
         tall[pl.ds(2 * n + 1, ROWS, stride=KT), :] = y[:, HEAD:]
 
-    @pl.loop(0, F // group, unroll=2)
+    @pl.loop(0, F // group, unroll=4)
     def _(i):
         first = pl.multiple_of(i * group, group)
         row = pl.multiple_of(first * KT, group * KT)
@@ -316,7 +325,7 @@
     def exchange(source, row_of, target, place, send, recv):
         pltpu.make_async_copy(source.at[row_of(me)], target.at[place], recv).start()
 
-        @pl.loop(1, count, unroll=7)
+        @pl.loop(1, count, unroll=21)
         def _(by):
             to = lax.rem(me + by * STRIDE, count)
             pltpu.make_async_remote_copy(
@@ -555,6 +564,9 @@
         def _(unit):
             send_back(unit)
 
+    gather.finish()
+    swap.wait_send()
+
     @pl.loop(0, VIDS)
     def _(vid):
         for pos in range(NP):
@@ -577,9 +589,6 @@
                 result[vid, :, k * HEAD : (k + 1) * HEAD] = tall[
                     pl.ds(tan * count * NP * KT + k, count * NP, stride=KT), :
                 ].astype(BF16)
-
-    gather.finish()
-    swap.wait_send()
 
     @pl.loop(0, UNITS)
     def _(unit):

time: 182 us -> 180 us (0.989)
  Pallas kernels: 177 us -> 175 us
where the time goes in v1:
time: 180 us; the launch traced here: 179 us
  Pallas kernels  175 us (97%)
  local copies, waits for them, and re-layouts  3.37 us (2%)
    pallas_call x1, Pallas kernels, shards(): pl.pallas_call(functools.partial(kernel, sizes, sections), out_shape=(res...  175 us

profile of v1, /device:TPU:7, one launch (start us, length us, event | category | flops | bytes accessed | tf_op | source)
XLA Modules:
  0.0 179.5 jit_solution(2134808990431809969)
XLA Ops:
  0.6 175.4 %blocks.1 = (bf16[2,128,2048]{2,1,0:T(8,128)(2,1)}, bf16[2,128,2048]{2,1,0:T(8,128)(2,1)}) custom-call(bf16[2,128,2048]{2,1,0:T(8,128)(2,1)} %bitcast.14, bf16[2,128,2048]{2,1,0:T(8,128)(2,1)} %bitcast.15, bf16[32,3072]{1,0:T(8,128)(2,1)} %bitcast.18, bf16[16,2048]{1,0:T(8,128)(2,1)} %bitcast.19, f32[2,128]{1,0:T(2,128)} %bitcast.23, s32[2]{0:T(128)} %index_ref.1, ...), custom_call_target="tpu_custom_call" | custom-call | tf_op jit(solution)/shard_map/blocks/pallas_call | solution.py:631
  176.1 0.0 copy-start
  176.1 2.4 %copy.15 = bf16[1,2,1,128,2048]{4,3,2,1,0:T(8,128)(2,1)} copy(bf16[1,2,1,128,2048]{4,3,2,1,0:T(8,128)(2,1)} %bitcast.17) | data formatting | bytes 2097152
  178.5 0.0 copy-done
  178.5 1.0 copy.16
Async XLA Ops:
  176.1 2.4 %copy-start = (bf16[2,128,2048]{2,1,0:T(8,128)(2,1)S(1)}, bf16[2,128,2048]{2,1,0:T(8,128)(2,1)}, u32[]{:S(2)}) copy-start(bf16[2,128,2048]{2,1,0:T(8,128)(2,1)} %get-tuple-element.5) | copy-start | bytes 3145732

commit v2 on v1

--- a/solution.py
+++ b/solution.py
@@ -351,8 +351,9 @@
         ).wait_send()
 
     leads = lax.rem(section, 2) == 0
+    video = section // 2
     loads = [
-        pltpu.make_async_copy(ref, plain.at[tan], load_sem.at[tan])
+        pltpu.make_async_copy(ref.at[video], plain.at[tan], load_sem.at[tan])
         for tan, ref in enumerate((x_ref, t_ref))
     ]
 
@@ -403,9 +404,12 @@
     swap.start()
     go("c", ("cy", 0))
 
-    def prepare(vid):
+    @pl.when(leads)
+    def _():
+        for load in loads:
+            load.wait()
         for tan in range(2):
-            spread(plain.at[tan, vid], tall, 0)
+            spread(plain.at[tan], tall, 0)
 
             @pl.loop(0, count // group)
             def _(i):
@@ -417,47 +421,42 @@
                     .reshape(group, NP, KT, HEAD)
                 )
                 for pos in range(NP):
-                    staged[vid * NP + pos, pl.ds(first, group), tan] = tiles[:, pos]
-
-    @pl.when(leads)
-    def _():
-        for load in loads:
-            load.wait()
-        prepare(0)
+                    staged[pos, pl.ds(first, group), tan] = tiles[:, pos]
 
     @pl.when(section == 0)
     def _():
-        exchange(
-            staged.at[0], lambda f: f, entering.at[0], me, x_send.at[0], x_recv.at[0]
-        )
-
-    def second_round(unit):
-        exchange(
-            staged.at[unit], flip, relay.at[unit], me, x_send.at[unit], x_recv.at[unit]
-        )
+        for pos in range(NP):
+            exchange(
+                staged.at[pos],
+                lambda f: f,
+                entering.at[pos],
+                me,
+                x_send.at[pos],
+                x_recv.at[pos],
+            )
 
     @pl.when(section == 2)
     def _():
-        second_round(1)
-        prepare(1)
-        second_round(2)
-        second_round(3)
-
-    def relayed(unit):
+        for pos in range(NP):
+            exchange(
+                staged.at[pos], flip, relay.at[pos], me, x_send.at[pos], x_recv.at[pos]
+            )
+
+    def relayed(pos):
         return pltpu.make_async_remote_copy(
-            src_ref=relay.at[unit],
-            dst_ref=entering.at[unit],
-            send_sem=relay_send.at[unit],
-            recv_sem=relay_recv.at[unit],
+            src_ref=relay.at[pos],
+            dst_ref=entering.at[NP + pos],
+            send_sem=relay_send.at[pos],
+            recv_sem=relay_recv.at[pos],
             device_id=(0, across),
             device_id_type=MESH,
         )
 
-    def pass_to_first(unit):
+    def pass_to_first(pos):
         @pl.when(section == 2)
         def _():
-            exchange_came(staged.at[unit], relay.at[unit], x_recv.at[unit])
-            relayed(unit).start()
+            exchange_came(staged.at[pos], relay.at[pos], x_recv.at[pos])
+            relayed(pos).start()
 
     for vid in range(VIDS):
         time_value = (index_ref[vid].astype(F32) + 0.5) * (math.pi / (2.0 * T_STEPS))
@@ -486,17 +485,16 @@
     go(("cy", 1), ("cx", 1), ("cy", 7), ("cx", 7), ("cy", 2), ("cy", 6))
     go("b", ("by", 2), ("by", 6))
     go("c", ("cy", 4))
-    pass_to_first(1)
+    pass_to_first(0)
     go(("az", 1), ("az", 3), ("by", 1), ("by", 7), ("az", 2))
     go(("cy", 2), ("cx", 2), ("cy", 6), ("cx", 6), ("cy", 3), ("cy", 5), ("cy", 4))
     go("b", ("by", 3), ("by", 5))
     go(("az", 0), ("by", 0), ("az", 1), ("az", 3))
     go(("cy", 3), ("cx", 3), ("cy", 5), ("cx", 5), ("cy", 4), ("cx", 4))
-    pass_to_first(2)
+    pass_to_first(1)
 
     go("b", ("by", 4))
     go(("by", 2), ("by", 6), ("az", 2), ("by", 1), ("by", 7), ("az", 0))
-    pass_to_first(3)
     go(("by", 3), ("by", 5), ("az", 1), ("az", 3), ("by", 4), ("az", 2))
     go(("by", 2), ("by", 6), ("az", 0), ("by", 3), ("by", 5))
     go(("az", 1), ("az", 3), ("by", 4), ("az", 2))
@@ -531,13 +529,15 @@
 
     @pl.loop(0, UNITS)
     def _(unit):
-        @pl.when(jnp.logical_and(section == 0, unit == 0))
+        pos = unit % NP
+
+        @pl.when(jnp.logical_and(section == 0, unit < NP))
         def _():
-            exchange_came(staged.at[0], entering.at[0], x_recv.at[0])
-
-        @pl.when(jnp.logical_and(section == 0, unit > 0))
+            exchange_came(staged.at[pos], entering.at[pos], x_recv.at[pos])
+
+        @pl.when(jnp.logical_and(section == 0, unit >= NP))
         def _():
-            relayed(unit).wait_recv()
+            relayed(pos).wait_recv()
 
         @pl.when(section > 0)
         def _():
@@ -600,20 +600,15 @@
         def _():
             onward(unit).wait_send()
 
-        @pl.when(
-            jnp.logical_or(
-                jnp.logical_and(section == 0, unit == 0),
-                jnp.logical_and(section == 2, unit > 0),
-            )
-        )
-        def _():
-            exchange_sent(
-                staged.at[unit], relay.at[unit], x_send.at[unit], x_recv.at[unit]
-            )
-
-        @pl.when(jnp.logical_and(section == 2, unit > 0))
-        def _():
-            relayed(unit).wait_send()
+    @pl.when(leads)
+    def _():
+        for pos in range(NP):
+            exchange_sent(staged.at[pos], relay.at[pos], x_send.at[pos], x_recv.at[pos])
+
+    @pl.when(section == 2)
+    def _():
+        for pos in range(NP):
+            relayed(pos).wait_send()
 
 
 def shards(sizes, x_in, x_tan, t_index, w_qkv, w_out, qk_gain, mod_amp, mod_freq, mod_phase):
@@ -639,9 +634,9 @@
             pltpu.VMEM((nz, nx, ny, ROWS_OUT, PACKED), BF16),
             pltpu.VMEM((VIDS, 3, KT, HEAD), F32),
             pltpu.VMEM((VIDS, 3, KT, HEAD), F32),
-            pltpu.VMEM((2, VIDS, places, D), BF16),
-            pltpu.VMEM(units, BF16),
-            pltpu.VMEM(units, BF16),
+            pltpu.VMEM((2, places, D), BF16),
+            pltpu.VMEM((NP,) + units[1:], BF16),
+            pltpu.VMEM((NP,) + units[1:], BF16),
             pltpu.VMEM(units, BF16),
             pltpu.VMEM(units, BF16),
             pltpu.VMEM(units, BF16),
@@ -654,10 +649,10 @@
             dma,
             dma((rings,)),
             dma((rings,)),
-            dma((UNITS,)),
-            dma((UNITS,)),
-            dma((UNITS,)),
-            dma((UNITS,)),
+            dma((NP,)),
+            dma((NP,)),
+            dma((NP,)),
+            dma((NP,)),
             dma((UNITS,)),
             dma((UNITS,)),
             dma((UNITS,)),

time: 180 us -> 183 us (1.017)
  Pallas kernels: 175 us -> 179 us
    pallas_call x1, Pallas kernels: 175 us -> 179 us  [shards(): pl.pallas_call(functools.partial(kernel, sizes, sections), out_shape=(res...]
where the time goes in v2:
time: 183 us
  Pallas kernels  179 us (98%)
  local copies, waits for them, and re-layouts  3.37 us (2%)
    pallas_call x1, Pallas kernels, shards(): pl.pallas_call(functools.partial(kernel, sizes, sections), out_shape=(res...  179 us

profile of v2, /device:TPU:7, one launch (start us, length us, event | category | flops | bytes accessed | tf_op | source)
XLA Modules:
  0.0 183.0 jit_solution(6636658130633829263)
XLA Ops:
  0.6 179.0 %blocks.1 = (bf16[2,128,2048]{2,1,0:T(8,128)(2,1)}, bf16[2,128,2048]{2,1,0:T(8,128)(2,1)}) custom-call(bf16[2,128,2048]{2,1,0:T(8,128)(2,1)} %bitcast.14, bf16[2,128,2048]{2,1,0:T(8,128)(2,1)} %bitcast.15, bf16[32,3072]{1,0:T(8,128)(2,1)} %bitcast.18, bf16[16,2048]{1,0:T(8,128)(2,1)} %bitcast.19, f32[2,128]{1,0:T(2,128)} %bitcast.23, s32[2]{0:T(128)} %index_ref.1, ...), custom_call_target="tpu_custom_call" | custom-call | tf_op jit(solution)/shard_map/blocks/pallas_call | solution.py:626
  179.6 0.0 copy-start
  179.6 2.4 %copy.15 = bf16[1,2,1,128,2048]{4,3,2,1,0:T(8,128)(2,1)} copy(bf16[1,2,1,128,2048]{4,3,2,1,0:T(8,128)(2,1)} %bitcast.17) | data formatting | bytes 2097152
  182.0 0.0 copy-done
  182.0 1.0 copy.16
Async XLA Ops:
  179.6 2.4 %copy-start = (bf16[2,128,2048]{2,1,0:T(8,128)(2,1)S(1)}, bf16[2,128,2048]{2,1,0:T(8,128)(2,1)}, u32[]{:S(2)}) copy-start(bf16[2,128,2048]{2,1,0:T(8,128)(2,1)} %get-tuple-element.5) | copy-start | bytes 3145732

commit v3 on v1

--- a/solution.py
+++ b/solution.py
@@ -28,7 +28,7 @@
 MESH = pl.DeviceIdType.MESH
 ROWS_OUT = 16
 PACKED = 2 * 3 * HD + D
-Z_LAST, Y_LAST = 2816, 5632
+Z_LAST, Y_LAST = 2304, 5376
 
 
 def timing(amp, freq, phase, time_value):
@@ -66,10 +66,9 @@
         )
 
     def start(self, piece, begin, width, sem, peer):
-        for part in range(2):
-            columns = pl.ds(begin + part * (width // 2), width // 2)
-            self.copy(piece(columns), sem, peer).start()
-        self.live.append(self.copy(piece(pl.ds(begin, width)), sem, peer))
+        copy = self.copy(piece(pl.ds(begin, width)), sem, peer)
+        copy.start()
+        self.live.append(copy)
 
     def ring(self, axis, first, stop, fixed, single=False):
         size = self.sizes[0] if axis == "z" else self.sizes[2]

time: 180 us -> 184 us (1.022)
  Pallas kernels: 175 us -> 180 us
    pallas_call x1, Pallas kernels: 175 us -> 180 us  [shards(): pl.pallas_call(functools.partial(kernel, sizes, sections), out_shape=(res...]
where the time goes in v3:
time: 184 us
  Pallas kernels  180 us (98%)
  local copies, waits for them, and re-layouts  3.37 us (2%)
    pallas_call x1, Pallas kernels, shards(): pl.pallas_call(functools.partial(kernel, sizes, sections), out_shape=(res...  180 us

profile of v3, /device:TPU:7, one launch (start us, length us, event | category | flops | bytes accessed | tf_op | source)
XLA Modules:
  0.0 183.9 jit_solution(8759387176336308546)
XLA Ops:
  0.6 179.9 %blocks.1 = (bf16[2,128,2048]{2,1,0:T(8,128)(2,1)}, bf16[2,128,2048]{2,1,0:T(8,128)(2,1)}) custom-call(bf16[2,128,2048]{2,1,0:T(8,128)(2,1)} %bitcast.14, bf16[2,128,2048]{2,1,0:T(8,128)(2,1)} %bitcast.15, bf16[32,3072]{1,0:T(8,128)(2,1)} %bitcast.18, bf16[16,2048]{1,0:T(8,128)(2,1)} %bitcast.19, f32[2,128]{1,0:T(2,128)} %bitcast.23, s32[2]{0:T(128)} %index_ref.1, ...), custom_call_target="tpu_custom_call" | custom-call | tf_op jit(solution)/shard_map/blocks/pallas_call | solution.py:630
  180.6 0.0 copy-start
  180.6 2.4 %copy.15 = bf16[1,2,1,128,2048]{4,3,2,1,0:T(8,128)(2,1)} copy(bf16[1,2,1,128,2048]{4,3,2,1,0:T(8,128)(2,1)} %bitcast.17) | data formatting | bytes 2097152
  183.0 0.0 copy-done
  183.0 1.0 copy.16
Async XLA Ops:
  180.6 2.4 %copy-start = (bf16[2,128,2048]{2,1,0:T(8,128)(2,1)S(1)}, bf16[2,128,2048]{2,1,0:T(8,128)(2,1)}, u32[]{:S(2)}) copy-start(bf16[2,128,2048]{2,1,0:T(8,128)(2,1)} %get-tuple-element.5) | copy-start | bytes 3145732

commit v4 on v3

--- a/solution.py
+++ b/solution.py
@@ -28,7 +28,7 @@
 MESH = pl.DeviceIdType.MESH
 ROWS_OUT = 16
 PACKED = 2 * 3 * HD + D
-Z_LAST, Y_LAST = 2304, 5376
+Z_LAST, Y_LAST = 2816, 5632
 
 
 def timing(amp, freq, phase, time_value):
@@ -551,7 +551,7 @@
             for part in range(HOP_PARTS):
                 onward(unit, part * (F // HOP_PARTS), F // HOP_PARTS).start()
 
-        @pl.when(section > 0)
+        @pl.when(section > 1)
         def _():
             send_back(unit)
 
@@ -559,6 +559,8 @@
     def _():
         pl.semaphore_wait(turn_sem, 1)
 
+    @pl.when(section < 2)
+    def _():
         @pl.loop(0, UNITS)
         def _(unit):
             send_back(unit)

time: 184 us -> 180 us (0.978)
  Pallas kernels: 180 us -> 175 us
    pallas_call x1, Pallas kernels: 180 us -> 175 us  [shards(): pl.pallas_call(functools.partial(kernel, sizes, sections), out_shape=(res...]
where the time goes in v4:
time: 180 us; the launch traced here: 179 us
  Pallas kernels  175 us (97%)
  local copies, waits for them, and re-layouts  3.37 us (2%)
    pallas_call x1, Pallas kernels, shards(): pl.pallas_call(functools.partial(kernel, sizes, sections), out_shape=(res...  175 us

profile of v4, /device:TPU:7, one launch (start us, length us, event | category | flops | bytes accessed | tf_op | source)
XLA Modules:
  0.0 179.5 jit_solution(13583321515892159855)
XLA Ops:
  0.6 175.4 %blocks.1 = (bf16[2,128,2048]{2,1,0:T(8,128)(2,1)}, bf16[2,128,2048]{2,1,0:T(8,128)(2,1)}) custom-call(bf16[2,128,2048]{2,1,0:T(8,128)(2,1)} %bitcast.14, bf16[2,128,2048]{2,1,0:T(8,128)(2,1)} %bitcast.15, bf16[32,3072]{1,0:T(8,128)(2,1)} %bitcast.18, bf16[16,2048]{1,0:T(8,128)(2,1)} %bitcast.19, f32[2,128]{1,0:T(2,128)} %bitcast.23, s32[2]{0:T(128)} %index_ref.1, ...), custom_call_target="tpu_custom_call" | custom-call | tf_op jit(solution)/shard_map/blocks/pallas_call | solution.py:632
  176.1 0.0 copy-start
  176.1 2.4 %copy.15 = bf16[1,2,1,128,2048]{4,3,2,1,0:T(8,128)(2,1)} copy(bf16[1,2,1,128,2048]{4,3,2,1,0:T(8,128)(2,1)} %bitcast.17) | data formatting | bytes 2097152
  178.5 0.0 copy-done
  178.5 1.0 copy.16
Async XLA Ops:
  176.1 2.4 %copy-start = (bf16[2,128,2048]{2,1,0:T(8,128)(2,1)S(1)}, bf16[2,128,2048]{2,1,0:T(8,128)(2,1)}, u32[]{:S(2)}) copy-start(bf16[2,128,2048]{2,1,0:T(8,128)(2,1)} %get-tuple-element.5) | copy-start | bytes 3145732

commit v5 on v4

--- a/solution.py
+++ b/solution.py
@@ -21,7 +21,6 @@
 ROWS = 2 * F
 HALF = F
 HOP_PARTS = 4
-STRIDE = 27
 EPS = 1e-06
 F32 = jnp.float32
 BF16 = jnp.bfloat16
@@ -286,6 +285,7 @@
     entering,
     leaving,
     returned,
+    carry,
     tall,
     flat,
     att,
@@ -303,6 +303,8 @@
     pass_recv,
     out_send,
     out_recv,
+    carry_send,
+    carry_recv,
     turn_sem,
 ):
     nz, nx, ny = sizes
@@ -321,12 +323,13 @@
     neighbour = (section, lax.rem(me + 1, count))
     group = 8
 
-    def exchange(source, row_of, target, place, send, recv):
-        pltpu.make_async_copy(source.at[row_of(me)], target.at[place], recv).start()
-
-        @pl.loop(1, count, unroll=21)
-        def _(by):
-            to = lax.rem(me + by * STRIDE, count)
+    plane = nx * ny
+    low = lax.rem(me, plane)
+    far = nz // 2
+
+    def exchange(source, row_of, target, place, send, recv, distances):
+        def one(distance, by):
+            to = lax.rem(z + distance + nz, nz) * plane + lax.rem(low + by, plane)
             pltpu.make_async_remote_copy(
                 src_ref=source.at[row_of(to)],
                 dst_ref=target.at[place],
@@ -335,6 +338,69 @@
                 device_id=(section, to),
                 device_id_type=MESH,
             ).start()
+
+        pltpu.make_async_copy(source.at[row_of(me)], target.at[place], recv).start()
+
+        @pl.loop(0, plane)
+        def _(by):
+            for distance in distances:
+                one(distance, by)
+
+        @pl.loop(1, plane)
+        def _(by):
+            one(0, by)
+
+    near = [sign * distance for distance in range(1, far) for sign in (1, -1)]
+
+    def carried(unit, way, ref):
+        to = lax.rem(z + (2 * way - 1) + nz, nz) * plane + low
+        return pltpu.make_async_remote_copy(
+            src_ref=ref,
+            dst_ref=carry.at[unit, way],
+            send_sem=out_send.at[unit],
+            recv_sem=carry_recv.at[unit, way],
+            device_id=(section, to),
+            device_id_type=MESH,
+        )
+
+    def send_back(unit):
+        for way in range(2):
+            row = lax.rem(z + far, nz) * plane + way * ny
+            carried(unit, way, leaving.at[unit, pl.ds(row, ny)]).start()
+        exchange(
+            leaving.at[unit],
+            lambda f: f,
+            returned.at[unit],
+            slot,
+            out_send.at[unit],
+            out_recv.at[unit],
+            near,
+        )
+
+    def carry_on(unit):
+        for way in range(2):
+            carried(unit, way, carry.at[unit, way]).wait_recv()
+            begun = lax.rem(z - (2 * way - 1) + nz, nz)
+            end = lax.rem(begun + far, nz)
+            for to_y in range(ny):
+                pltpu.make_async_remote_copy(
+                    src_ref=carry.at[unit, way, to_y],
+                    dst_ref=returned.at[unit, slot + (begun - z) * plane],
+                    send_sem=carry_send.at[unit],
+                    recv_sem=out_recv.at[unit],
+                    device_id=(section, end * plane + way * ny + to_y),
+                    device_id_type=MESH,
+                ).start()
+
+    def carried_on(unit):
+        pltpu.make_async_remote_copy(
+            src_ref=carry.at[unit],
+            dst_ref=carry.at[unit],
+            send_sem=carry_send.at[unit],
+            recv_sem=carry_recv.at[unit, 0],
+            device_id=neighbour,
+            device_id_type=MESH,
+        ).wait_send()
 
     def exchange_came(source, target, recv):
         pltpu.make_async_copy(source, target, recv).wait()
@@ -427,12 +493,24 @@
     @pl.when(section == 0)
     def _():
         exchange(
-            staged.at[0], lambda f: f, entering.at[0], me, x_send.at[0], x_recv.at[0]
+            staged.at[0],
+            lambda f: f,
+            entering.at[0],
+            me,
+            x_send.at[0],
+            x_recv.at[0],
+            near + [far],
         )
 
     def second_round(unit):
         exchange(
-            staged.at[unit], flip, relay.at[unit], me, x_send.at[unit], x_recv.at[unit]
+            staged.at[unit],
+            flip,
+            relay.at[unit],
+            me,
+            x_send.at[unit],
+            x_recv.at[unit],
+            near + [far],
         )
 
     @pl.when(section == 2)
@@ -518,16 +596,6 @@
             device_id_type=MESH,
         )
 
-    def send_back(unit):
-        exchange(
-            leaving.at[unit],
-            lambda f: f,
-            returned.at[unit],
-            slot,
-            out_send.at[unit],
-            out_recv.at[unit],
-        )
-
     @pl.loop(0, UNITS)
     def _(unit):
         @pl.when(jnp.logical_and(section == 0, unit == 0))
@@ -555,6 +623,10 @@
         def _():
             send_back(unit)
 
+        @pl.when(jnp.logical_and(section > 1, unit > 0))
+        def _():
+            carry_on(unit - 1)
+
     @pl.when(section == 0)
     def _():
         pl.semaphore_wait(turn_sem, 1)
@@ -564,6 +636,12 @@
         @pl.loop(0, UNITS)
         def _(unit):
             send_back(unit)
+
+        @pl.loop(0, UNITS - 1)
+        def _(unit):
+            carry_on(unit)
+
+    carry_on(UNITS - 1)
 
     gather.finish()
     swap.wait_send()
@@ -596,6 +674,7 @@
         exchange_sent(
             leaving.at[unit], returned.at[unit], out_send.at[unit], out_recv.at[unit]
         )
+        carried_on(unit)
 
         @pl.when(section < sections - 1)
         def _():
@@ -646,6 +725,7 @@
             pltpu.VMEM(units, BF16),
             pltpu.VMEM(units, BF16),
             pltpu.VMEM(units, BF16),
+            pltpu.VMEM((UNITS, 2, ny, 2, KT, HEAD), BF16),
             pltpu.VMEM((2 * places * KT, HEAD), F32),
             pltpu.VMEM((ROWS, D), BF16),
             pltpu.VMEM((ROWS, HD), BF16),
@@ -663,6 +743,8 @@
             dma((UNITS,)),
             dma((UNITS,)),
             dma((UNITS,)),
+            dma((UNITS,)),
+            dma((UNITS, 2)),
             pltpu.SemaphoreType.REGULAR,
         ],
         compiler_params=pltpu.CompilerParams(

time: 180 us -> 180 us (level)
  no operation moved by 1% of the time
where the time goes in v5:
time: 180 us
  Pallas kernels  176 us (98%)
  local copies, waits for them, and re-layouts  3.37 us (2%)
    pallas_call x1, Pallas kernels, shards(): pl.pallas_call(functools.partial(kernel, sizes, sections), out_shape=(res...  176 us

profile of v5, /device:TPU:7, one launch (start us, length us, event | category | flops | bytes accessed | tf_op | source)
XLA Modules:
  0.0 180.0 jit_solution(9779501085116126490)
XLA Ops:
  0.6 176.0 %blocks.1 = (bf16[2,128,2048]{2,1,0:T(8,128)(2,1)}, bf16[2,128,2048]{2,1,0:T(8,128)(2,1)}) custom-call(bf16[2,128,2048]{2,1,0:T(8,128)(2,1)} %bitcast.14, bf16[2,128,2048]{2,1,0:T(8,128)(2,1)} %bitcast.15, bf16[32,3072]{1,0:T(8,128)(2,1)} %bitcast.18, bf16[16,2048]{1,0:T(8,128)(2,1)} %bitcast.19, f32[2,128]{1,0:T(2,128)} %bitcast.23, s32[2]{0:T(128)} %index_ref.1, ...), custom_call_target="tpu_custom_call" | custom-call | tf_op jit(solution)/shard_map/blocks/pallas_call | solution.py:711
  176.6 0.0 copy-start
  176.6 2.4 %copy.15 = bf16[1,2,1,128,2048]{4,3,2,1,0:T(8,128)(2,1)} copy(bf16[1,2,1,128,2048]{4,3,2,1,0:T(8,128)(2,1)} %bitcast.17) | data formatting | bytes 2097152
  179.0 0.0 copy-done
  179.0 1.0 copy.16
Async XLA Ops:
  176.6 2.4 %copy-start = (bf16[2,128,2048]{2,1,0:T(8,128)(2,1)S(1)}, bf16[2,128,2048]{2,1,0:T(8,128)(2,1)}, u32[]{:S(2)}) copy-start(bf16[2,128,2048]{2,1,0:T(8,128)(2,1)} %get-tuple-element.5) | copy-start | bytes 3145732

commit v6 on v4

--- a/solution.py
+++ b/solution.py
@@ -188,9 +188,7 @@
     return mixed[:HALF], mixed[HALF:] + jnp.dot(prob, dvalue, preferred_element_type=F32)
 
 
-def block_step(
-    unit, entering, leaving, weights, gains_ref, mods_ref, dmods_ref, tall, flat, att
-):
+def modulate(unit, entering, mods_ref, dmods_ref, tall, flat):
     group = 8
     vid = unit // NP
 
@@ -218,6 +216,13 @@
 
     for k in range(KT):
         flat[:, k * HEAD : (k + 1) * HEAD] = tall[pl.ds(k, ROWS, stride=KT), :].astype(BF16)
+
+
+def block_step(
+    unit, entering, leaving, weights, gains_ref, mods_ref, dmods_ref, tall, flat, att
+):
+    group = 8
+    vid = unit // NP
 
     def third(number, pair):
         column = number * HD + pair * 2 * HEAD
@@ -401,6 +406,8 @@
     )
     swap.start()
     go("c", ("cy", 0))
+    swapped.wait_recv()
+    go("b", "a", ("by", 0), ("az", 0))
 
     def prepare(vid):
         for tan in range(2):
@@ -464,8 +471,6 @@
             amp_ref[...], freq_ref[...], phase_ref[...], time_value
         )
 
-    swapped.wait_recv()
-    go("b", "a", ("by", 0), ("az", 0))
     go("c", ("cy", 1), ("cy", 7))
     go("a", ("az", 1), ("az", 3))
     go(("cy", 0),)
@@ -497,14 +502,6 @@
     go(("by", 2), ("by", 6), ("az", 2), ("by", 1), ("by", 7), ("az", 0))
     pass_to_first(3)
     go(("by", 3), ("by", 5), ("az", 1), ("az", 3), ("by", 4), ("az", 2))
-    go(("by", 2), ("by", 6), ("az", 0), ("by", 3), ("by", 5))
-    go(("az", 1), ("az", 3), ("by", 4), ("az", 2))
-    go(*(("cx", by) for by in range(nz)))
-
-    @pl.when(section == 1)
-    def _():
-        pl.semaphore_signal(turn_sem, inc=1, device_id=(0, me), device_id_type=MESH)
-
     def onward(unit, first=0, frames=F):
         return pltpu.make_async_remote_copy(
             src_ref=leaving.at[unit, pl.ds(first, frames)],
@@ -518,6 +515,33 @@
             device_id_type=MESH,
         )
 
+    def take_in(unit):
+        @pl.when(jnp.logical_and(section == 0, unit == 0))
+        def _():
+            exchange_came(staged.at[0], entering.at[0], x_recv.at[0])
+
+        @pl.when(jnp.logical_and(section == 0, unit > 0))
+        def _():
+            relayed(unit).wait_recv()
+
+        @pl.when(section > 0)
+        def _():
+            onward(unit).wait_recv()
+
+        modulate(unit, entering, mods_ref, dmods_ref, tall, flat)
+
+    @pl.when(first_half)
+    def _():
+        take_in(0)
+
+    go(("by", 2), ("by", 6), ("az", 0), ("by", 3), ("by", 5))
+    go(("az", 1), ("az", 3), ("by", 4), ("az", 2))
+    go(*(("cx", by) for by in range(nz)))
+
+    @pl.when(section == 1)
+    def _():
+        pl.semaphore_signal(turn_sem, inc=1, device_id=(0, me), device_id_type=MESH)
+
     def send_back(unit):
         exchange(
             leaving.at[unit],
@@ -530,17 +554,9 @@
 
     @pl.loop(0, UNITS)
     def _(unit):
-        @pl.when(jnp.logical_and(section == 0, unit == 0))
-        def _():
-            exchange_came(staged.at[0], entering.at[0], x_recv.at[0])
-
-        @pl.when(jnp.logical_and(section == 0, unit > 0))
-        def _():
-            relayed(unit).wait_recv()
-
-        @pl.when(section > 0)
-        def _():
-            onward(unit).wait_recv()
+        @pl.when(jnp.logical_or(jnp.logical_not(first_half), unit > 0))
+        def _():
+            take_in(unit)
 
         block_step(
             unit, entering, leaving, weights, gains_ref, mods_ref, dmods_ref, tall, flat, att

time: 180 us -> 181 us (level)
  Pallas kernels: 175 us -> 177 us
where the time goes in v6:
time: 181 us
  Pallas kernels  177 us (98%)
  local copies, waits for them, and re-layouts  3.37 us (2%)
    pallas_call x1, Pallas kernels, shards(): pl.pallas_call(functools.partial(kernel, sizes, sections), out_shape=(res...  177 us

profile of v6, /device:TPU:7, one launch (start us, length us, event | category | flops | bytes accessed | tf_op | source)
XLA Modules:
  0.0 180.8 jit_solution(2328776091531326180)
XLA Ops:
  0.6 176.8 %blocks.1 = (bf16[2,128,2048]{2,1,0:T(8,128)(2,1)}, bf16[2,128,2048]{2,1,0:T(8,128)(2,1)}) custom-call(bf16[2,128,2048]{2,1,0:T(8,128)(2,1)} %bitcast.14, bf16[2,128,2048]{2,1,0:T(8,128)(2,1)} %bitcast.15, bf16[32,3072]{1,0:T(8,128)(2,1)} %bitcast.18, bf16[16,2048]{1,0:T(8,128)(2,1)} %bitcast.19, f32[2,128]{1,0:T(2,128)} %bitcast.23, s32[2]{0:T(128)} %index_ref.1, ...), custom_call_target="tpu_custom_call" | custom-call | tf_op jit(solution)/shard_map/blocks/pallas_call | solution.py:648
  177.5 0.0 copy-start
  177.5 2.4 %copy.15 = bf16[1,2,1,128,2048]{4,3,2,1,0:T(8,128)(2,1)} copy(bf16[1,2,1,128,2048]{4,3,2,1,0:T(8,128)(2,1)} %bitcast.17) | data formatting | bytes 2097152
  179.9 0.0 copy-done
  179.9 1.0 copy.16
Async XLA Ops:
  177.5 2.4 %copy-start = (bf16[2,128,2048]{2,1,0:T(8,128)(2,1)S(1)}, bf16[2,128,2048]{2,1,0:T(8,128)(2,1)}, u32[]{:S(2)}) copy-start(bf16[2,128,2048]{2,1,0:T(8,128)(2,1)} %get-tuple-element.5) | copy-start | bytes 3145732

commit v7 on v4

--- a/solution.py
+++ b/solution.py
@@ -20,7 +20,7 @@
 UNITS = VIDS * NP
 ROWS = 2 * F
 HALF = F
-HOP_PARTS = 4
+HOP_PARTS = 16
 STRIDE = 27
 EPS = 1e-06
 F32 = jnp.float32

time: 180 us -> 180 us (level)
  no operation moved by 1% of the time
where the time goes in v7:
time: 180 us
  Pallas kernels  176 us (98%)
  local copies, waits for them, and re-layouts  3.37 us (2%)
    pallas_call x1, Pallas kernels, shards(): pl.pallas_call(functools.partial(kernel, sizes, sections), out_shape=(res...  176 us

profile of v7, /device:TPU:7, one launch (start us, length us, event | category | flops | bytes accessed | tf_op | source)
XLA Modules:
  0.0 179.6 jit_solution(13109314484435004164)
XLA Ops:
  0.6 175.5 %blocks.1 = (bf16[2,128,2048]{2,1,0:T(8,128)(2,1)}, bf16[2,128,2048]{2,1,0:T(8,128)(2,1)}) custom-call(bf16[2,128,2048]{2,1,0:T(8,128)(2,1)} %bitcast.14, bf16[2,128,2048]{2,1,0:T(8,128)(2,1)} %bitcast.15, bf16[32,3072]{1,0:T(8,128)(2,1)} %bitcast.18, bf16[16,2048]{1,0:T(8,128)(2,1)} %bitcast.19, f32[2,128]{1,0:T(2,128)} %bitcast.23, s32[2]{0:T(128)} %index_ref.1, ...), custom_call_target="tpu_custom_call" | custom-call | tf_op jit(solution)/shard_map/blocks/pallas_call | solution.py:632
  176.2 0.0 copy-start
  176.2 2.4 %copy.15 = bf16[1,2,1,128,2048]{4,3,2,1,0:T(8,128)(2,1)} copy(bf16[1,2,1,128,2048]{4,3,2,1,0:T(8,128)(2,1)} %bitcast.17) | data formatting | bytes 2097152
  178.6 0.0 copy-done
  178.6 1.0 copy.16
Async XLA Ops:
  176.2 2.4 %copy-start = (bf16[2,128,2048]{2,1,0:T(8,128)(2,1)S(1)}, bf16[2,128,2048]{2,1,0:T(8,128)(2,1)}, u32[]{:S(2)}) copy-start(bf16[2,128,2048]{2,1,0:T(8,128)(2,1)} %get-tuple-element.5) | copy-start | bytes 3145732

commit v8 on v4

--- a/solution.py
+++ b/solution.py
@@ -355,7 +355,7 @@
         for tan, ref in enumerate((x_ref, t_ref))
     ]
 
-    @pl.when(leads)
+    @pl.when(section == 2)
     def _():
         for load in loads:
             load.start()
@@ -418,29 +418,21 @@
                 for pos in range(NP):
                     staged[vid * NP + pos, pl.ds(first, group), tan] = tiles[:, pos]
 
-    @pl.when(leads)
+    @pl.when(section == 2)
     def _():
         for load in loads:
             load.wait()
-        prepare(0)
-
-    @pl.when(section == 0)
-    def _():
-        exchange(
-            staged.at[0], lambda f: f, entering.at[0], me, x_send.at[0], x_recv.at[0]
-        )
-
-    def second_round(unit):
-        exchange(
-            staged.at[unit], flip, relay.at[unit], me, x_send.at[unit], x_recv.at[unit]
-        )
-
-    @pl.when(section == 2)
-    def _():
-        second_round(1)
-        prepare(1)
-        second_round(2)
-        second_round(3)
+        for vid in range(VIDS):
+            prepare(vid)
+            for unit in range(vid * NP, vid * NP + NP):
+                exchange(
+                    staged.at[unit],
+                    flip,
+                    relay.at[unit],
+                    me,
+                    x_send.at[unit],
+                    x_recv.at[unit],
+                )
 
     def relayed(unit):
         return pltpu.make_async_remote_copy(
@@ -485,6 +477,7 @@
     go(("cy", 1), ("cx", 1), ("cy", 7), ("cx", 7), ("cy", 2), ("cy", 6))
     go("b", ("by", 2), ("by", 6))
     go("c", ("cy", 4))
+    pass_to_first(0)
     pass_to_first(1)
     go(("az", 1), ("az", 3), ("by", 1), ("by", 7), ("az", 2))
     go(("cy", 2), ("cx", 2), ("cy", 6), ("cx", 6), ("cy", 3), ("cy", 5), ("cy", 4))
@@ -530,11 +523,7 @@
 
     @pl.loop(0, UNITS)
     def _(unit):
-        @pl.when(jnp.logical_and(section == 0, unit == 0))
-        def _():
-            exchange_came(staged.at[0], entering.at[0], x_recv.at[0])
-
-        @pl.when(jnp.logical_and(section == 0, unit > 0))
+        @pl.when(section == 0)
         def _():
             relayed(unit).wait_recv()
 
@@ -601,19 +590,11 @@
         def _():
             onward(unit).wait_send()
 
-        @pl.when(
-            jnp.logical_or(
-                jnp.logical_and(section == 0, unit == 0),
-                jnp.logical_and(section == 2, unit > 0),
-            )
-        )
+        @pl.when(section == 2)
         def _():
             exchange_sent(
                 staged.at[unit], relay.at[unit], x_send.at[unit], x_recv.at[unit]
             )
-
-        @pl.when(jnp.logical_and(section == 2, unit > 0))
-        def _():
             relayed(unit).wait_send()
 
 

time: 180 us -> 177 us (0.983)
  Pallas kernels: 175 us -> 173 us
    pallas_call x1, Pallas kernels: 175 us -> 173 us  [shards(): pl.pallas_call(functools.partial(kernel, sizes, sections), out_shape=(res...]
where the time goes in v8:
time: 177 us
  Pallas kernels  173 us (98%)
  local copies, waits for them, and re-layouts  3.37 us (2%)
    pallas_call x1, Pallas kernels, shards(): pl.pallas_call(functools.partial(kernel, sizes, sections), out_shape=(res...  173 us

profile of v8, /device:TPU:7, one launch (start us, length us, event | category | flops | bytes accessed | tf_op | source)
XLA Modules:
  0.0 176.8 jit_solution(3478720241906481204)
XLA Ops:
  0.6 172.8 %blocks.1 = (bf16[2,128,2048]{2,1,0:T(8,128)(2,1)}, bf16[2,128,2048]{2,1,0:T(8,128)(2,1)}) custom-call(bf16[2,128,2048]{2,1,0:T(8,128)(2,1)} %bitcast.14, bf16[2,128,2048]{2,1,0:T(8,128)(2,1)} %bitcast.15, bf16[32,3072]{1,0:T(8,128)(2,1)} %bitcast.18, bf16[16,2048]{1,0:T(8,128)(2,1)} %bitcast.19, f32[2,128]{1,0:T(2,128)} %bitcast.23, s32[2]{0:T(128)} %index_ref.1, ...), custom_call_target="tpu_custom_call" | custom-call | tf_op jit(solution)/shard_map/blocks/pallas_call | solution.py:613
  173.4 0.0 copy-start
  173.4 2.4 %copy.15 = bf16[1,2,1,128,2048]{4,3,2,1,0:T(8,128)(2,1)} copy(bf16[1,2,1,128,2048]{4,3,2,1,0:T(8,128)(2,1)} %bitcast.17) | data formatting | bytes 2097152
  175.8 0.0 copy-done
  175.8 1.0 copy.16
Async XLA Ops:
  173.4 2.4 %copy-start = (bf16[2,128,2048]{2,1,0:T(8,128)(2,1)S(1)}, bf16[2,128,2048]{2,1,0:T(8,128)(2,1)}, u32[]{:S(2)}) copy-start(bf16[2,128,2048]{2,1,0:T(8,128)(2,1)} %get-tuple-element.5) | copy-start | bytes 3145732

commit v9 on v8

--- a/solution.py
+++ b/solution.py
@@ -194,7 +194,7 @@
     group = 8
     vid = unit // NP
 
-    @pl.loop(0, F // group, unroll=4)
+    @pl.loop(0, F // group, unroll=8)
     def _(i):
         first = pl.multiple_of(i * group, group)
         hidden = entering[unit, pl.ds(first, group), 0].astype(F32)
@@ -249,7 +249,7 @@
         tall[pl.ds(2 * n, ROWS, stride=KT), :] = y[:, :HEAD]
         tall[pl.ds(2 * n + 1, ROWS, stride=KT), :] = y[:, HEAD:]
 
-    @pl.loop(0, F // group, unroll=4)
+    @pl.loop(0, F // group, unroll=8)
     def _(i):
         first = pl.multiple_of(i * group, group)
         row = pl.multiple_of(first * KT, group * KT)
@@ -563,7 +563,7 @@
             unit = vid * NP + pos
             exchange_came(leaving.at[unit], returned.at[unit], out_recv.at[unit])
 
-            @pl.loop(0, count // group)
+            @pl.loop(0, count // group, unroll=4)
             def _(i):
                 first = pl.multiple_of(i * group, group)
                 for tan in range(2):

time: 177 us -> 177 us (level)
  no operation moved by 1% of the time
where the time goes in v9:
time: 177 us
  Pallas kernels  173 us (98%)
  local copies, waits for them, and re-layouts  3.37 us (2%)
    pallas_call x1, Pallas kernels, shards(): pl.pallas_call(functools.partial(kernel, sizes, sections), out_shape=(res...  173 us

profile of v9, /device:TPU:7, one launch (start us, length us, event | category | flops | bytes accessed | tf_op | source)
XLA Modules:
  0.0 176.7 jit_solution(4542169544764492735)
XLA Ops:
  0.6 172.6 %blocks.1 = (bf16[2,128,2048]{2,1,0:T(8,128)(2,1)}, bf16[2,128,2048]{2,1,0:T(8,128)(2,1)}) custom-call(bf16[2,128,2048]{2,1,0:T(8,128)(2,1)} %bitcast.14, bf16[2,128,2048]{2,1,0:T(8,128)(2,1)} %bitcast.15, bf16[32,3072]{1,0:T(8,128)(2,1)} %bitcast.18, bf16[16,2048]{1,0:T(8,128)(2,1)} %bitcast.19, f32[2,128]{1,0:T(2,128)} %bitcast.23, s32[2]{0:T(128)} %index_ref.1, ...), custom_call_target="tpu_custom_call" | custom-call | tf_op jit(solution)/shard_map/blocks/pallas_call | solution.py:613
  173.3 0.0 copy-start
  173.3 2.4 %copy.15 = bf16[1,2,1,128,2048]{4,3,2,1,0:T(8,128)(2,1)} copy(bf16[1,2,1,128,2048]{4,3,2,1,0:T(8,128)(2,1)} %bitcast.17) | data formatting | bytes 2097152
  175.7 0.0 copy-done
  175.7 1.0 copy.16
Async XLA Ops:
  173.3 2.4 %copy-start = (bf16[2,128,2048]{2,1,0:T(8,128)(2,1)S(1)}, bf16[2,128,2048]{2,1,0:T(8,128)(2,1)}, u32[]{:S(2)}) copy-start(bf16[2,128,2048]{2,1,0:T(8,128)(2,1)} %get-tuple-element.5) | copy-start | bytes 3145732
